TPU v7x, 32 devices: a whole 2x2x4 slice. The times are simulated.
32 devices in a mesh: fsdp: 8 (over y, x, core), rep: 4 (over z).
Axes of the slice: x: 2, y: 2, z: 4, core: 2. Of those that a mesh axis runs over, the one named last changes fastest.
Arguments:
- tokens: bfloat16 [12288, 1600], P(('fsdp', 'rep')), may hold values from -41 to 41
- norm_gain: float32 [1600], replicated, may hold values from 0.1 to 1.9
- up_weight: bfloat16 [6400, 1600], P('fsdp'), may hold values from -0.15625 to 0.15625
- up_bias: bfloat16 [6400], P('fsdp'), may hold values from -3 to 3
- keep_mask: int32 [128], P(('fsdp', 'rep')), may hold values 0 or 1
- cotangent: bfloat16 [12288, 6400], P(('fsdp', 'rep')), may hold values from -6 to 6
Outputs:
- hidden: bfloat16 [12288, 6400], P(('fsdp', 'rep'))
- grad_in: bfloat16 [12288, 1600], P(('fsdp', 'rep'))
- grad_weight: float32 [6400, 1600], P('fsdp')
- grad_bias: float32 [6400], P('fsdp')
- grad_gain: float32 [1600], replicated
All inputs are finite; a program needn't handle non-finite values. No bound on the sum of `keep_mask` on one device may be relied on, other than what follows from the above.
Results may differ from a plain program's by a relative error of at most 0.02.
Values may be sent and summed in bfloat16 or wider, within the bound.
No kernel may reach another device: no remote copies, remote signals or barrier semaphores. Data moves between devices by JAX's collectives and lax.ppermute only.
A program may use at most 192 MiB of HBM per device.

v0:
```python
import math

import jax
import jax.numpy as jnp
from jax import lax
from jax.sharding import PartitionSpec as P


def normalize(tokens, norm_gain):
    values = tokens.astype(jnp.float32)
    mean_sq = jnp.mean(values * values, axis=1, keepdims=True)
    inv_rms = lax.rsqrt(mean_sq + 1e-06)
    x_hat = values * inv_rms
    return (x_hat, inv_rms, (x_hat * norm_gain[None, :]).astype(jnp.bfloat16))


def activate(preact):
    cdf = 0.5 * (1.0 + jax.scipy.special.erf(preact * 0.7071067811865476))
    density = jnp.exp(-0.5 * preact * preact) * 0.3989422804014327
    return (preact * cdf, cdf + preact * density)


def row_scales(keep_mask, total_rows):
    per_sample = keep_mask.astype(jnp.float32) * (4.0 / 3.0)
    return jnp.repeat(per_sample, total_rows // keep_mask.shape[0])


def contract_last(left, right):
    return lax.dot_general(
        left, right, (((1,), (1,)), ((), ())), preferred_element_type=jnp.float32
    )


def local(tokens, norm_gain, up_weight, up_bias, keep_mask, cotangent):
    x_hat, inv_rms, normed = normalize(tokens, norm_gain)
    rows = tokens.shape[0]
    width = up_weight.shape[0]
    tok_total = rows * lax.axis_size("fsdp") * lax.axis_size("rep")
    inv_root = 1.0 / math.sqrt(tok_total)
    weight_all, bias_all = (
        lax.all_gather(up_weight, "fsdp", axis=0, tiled=True),
        lax.all_gather(up_bias, "fsdp", axis=0, tiled=True),
    )
    scales = row_scales(keep_mask, rows)[:, None]
    preact = contract_last(normed, weight_all) + bias_all.astype(jnp.float32)[None, :]
    gelu_out, slopes = activate(preact)
    hidden = (gelu_out * scales).astype(jnp.bfloat16)
    grad_pre = cotangent.astype(jnp.float32) * scales * slopes
    grad_low = grad_pre.astype(jnp.bfloat16)
    weight_part = lax.psum_scatter(
        lax.dot_general(
            grad_low, normed, (((0,), (0,)), ((), ())), preferred_element_type=jnp.float32
        ).astype(jnp.bfloat16),
        "fsdp",
        scatter_dimension=0,
        tiled=True,
    )
    weight_sum = lax.psum(weight_part, "rep").astype(jnp.float32)
    grad_norm = jnp.dot(grad_low, weight_all, preferred_element_type=jnp.float32)
    bias_total, gain_total = lax.psum(
        (jnp.sum(grad_pre, axis=0), jnp.sum(grad_norm * x_hat, axis=0)), ("fsdp", "rep")
    )
    bias_sum = lax.dynamic_slice_in_dim(bias_total, lax.axis_index("fsdp") * width, width, 0)
    scaled = grad_norm * norm_gain[None, :]
    grad_in = (inv_rms * (scaled - x_hat * jnp.mean(scaled * x_hat, axis=1, keepdims=True))).astype(
        jnp.bfloat16
    )
    return (hidden, grad_in, weight_sum * inv_root, bias_sum * inv_root, gain_total * inv_root)


def solution(mesh):
    return jax.shard_map(
        local,
        mesh=mesh,
        in_specs=(
            P(("fsdp", "rep"), None),
            P(),
            P("fsdp", None),
            P("fsdp"),
            P(("fsdp", "rep")),
            P(("fsdp", "rep"), None),
        ),
        out_specs=(
            P(("fsdp", "rep"), None),
            P(("fsdp", "rep"), None),
            P("fsdp", None),
            P("fsdp"),
            P(),
        ),
        check_vma=False,
    )
```

profile of v0, /device:TPU:0, one launch (start us, length us, event | category | flops | bytes accessed | tf_op | source)
XLA Modules:
  0.0 425.2 jit_solution(13495270397967657912)
XLA Ops:
  7.2 0.0 all-gather.2.cloned.1.call-start
  7.2 0.7 all-gather.2.cloned.1.call-update
  7.9 0.0 reduce-scatter.2.cloned.1.call-start
  8.0 0.7 convert_multiply_fusion.3
  8.6 0.1 broadcast_in_dim.2
  8.7 0.1 mul.132
  8.8 1.2 dynamic-slice
  10.7 0.9 dynamic-update-slice
  11.5 26.0 %all-reduce = bf16[6400]{0:T(1024)(128)(2,1)S(1)} all-reduce(bf16[6400]{0:T(1024)(128)(2,1)S(1)} %dynamic-update-slice), channel_id=1, replica_groups=mesh['fsdp'=8,'rep'=4] {'fsdp'}, use_global_device_ids=true, to_apply=%add | all-reduce | flops 6400 | bytes 25600
  37.6 1.6 fusion.15
  39.2 82.5 %all-gather.2.cloned.1.call-done = bf16[6400,1600]{1,0:T(8,128)(2,1)} async-done(((bf16[800,1600]{1,0:T(8,128)(2,1)}), bf16[6400,1600]{1,0:T(8,128)(2,1)}) %all-gather.2.cloned.1.call-update) | async-done | bytes 20480016 | tf_op jit(solution)/shard_map/all_gather | solution.py:41
  121.7 19.9 %fusion.21 = (f32[6400]{0:T(1024)S(1)}, bf16[384,6400]{1,0:T(8,128)(2,1)}, bf16[384,6400]{1,0:T(8,128)(2,1)}) fusion(f32[384]{0:T(512)S(1)} %mul.132, bf16[384,6400]{1,0:T(8,128)(2,1)} %param.11, f32[6400]{0:T(1024)S(1)} %convert_element_type.32, bf16[6400,1600]{1,0:T(8,128)(2,1)} %all-gather.2.cloned.1.call-done, bf16[384,1600]{0,1:T(8,128)(2,1)} %param.6, ...), kind=kOutput, calls=%fused_computation.32 | convolution fusion | flops 7908550656 | bytes 36515072 | tf_op jit(solution)/shard_map/dot_general | solution.py:29
  141.6 17.7 %convolution_convert_fusion = bf16[6400,1600]{1,0:T(8,128)(2,1)} fusion(bf16[384,6400]{1,0:T(8,128)(2,1)} %get-tuple-element.10, bf16[384,1600]{0,1:T(8,128)(2,1)S(1)} %copy-done, f32[1600]{0:T(1024)S(1)} %copy-done.1, f32[384]{0:T(512)S(1)} %add_rsqrt_fusion), kind=kOutput, calls=%fused_computation | convolution fusion | flops 7877017600 | bytes 26631936 | tf_op jit(solution)/shard_map/dot_general | solution.py:51
  159.4 0.0 reduce-scatter.2.cloned.1.call-update
  159.4 0.2 all-reduce.4.cloned.1.call-start
  159.6 145.3 %reduce-scatter.2.cloned.1.call-done = bf16[800,1600]{1,0:T(8,128)(2,1)} async-done(((bf16[6400,1600]{1,0:T(8,128)(2,1)}), bf16[800,1600]{1,0:T(8,128)(2,1)}) %reduce-scatter.2.cloned.1.call-update) | async-done | bytes 2560016 | tf_op jit(solution)/shard_map/reduce_scatter | solution.py:50
  304.9 0.0 all-reduce.4.cloned.1.call-update
  305.0 18.3 %fusion.14 = (f32[1600]{0:T(1024)S(1)}, f32[384]{0:T(512)S(1)}, f32[384,1600]{0,1:T(8,128)}) fusion(bf16[384,1600]{0,1:T(8,128)(2,1)S(1)} %copy-done, f32[384]{0:T(512)S(1)} %add_rsqrt_fusion, f32[1600]{0:T(1024)S(1)} %copy-done.1, bf16[6400,1600]{1,0:T(8,128)(2,1)} %all-gather.2.cloned.1.call-done, bf16[384,6400]{1,0:T(8,128)(2,1)} %get-tuple-element.10), kind=kOutput, calls=%fused_computation.22 | convolution fusion | flops 7868618752 | bytes 29097472 | tf_op jit(solution)/shard_map/dot_general | solution.py:59
  323.3 44.5 %all-reduce.1 = (f32[6400]{0:T(1024)S(1)}, f32[1600]{0:T(1024)S(1)}) all-reduce(f32[6400]{0:T(1024)S(1)} %get-tuple-element.9, f32[1600]{0:T(1024)S(1)} %get-tuple-element.5), channel_id=1, replica_groups=mesh['fsdp'=8,'rep'=4] {'fsdp','rep'}, use_global_device_ids=true, to_apply=%region_5.0 | all-reduce | flops 8000 | bytes 64000 | tf_op jit(solution)/shard_map/psum | solution.py:60
  367.8 0.7 dynamic-slice_multiply_fusion
  368.5 0.6 broadcast_multiply_fusion
  369.1 3.3 fusion.13
  372.4 41.6 %all-reduce.4.cloned.1.call-done = bf16[800,1600]{1,0:T(8,128)(2,1)} async-done(((bf16[800,1600]{1,0:T(8,128)(2,1)}), bf16[800,1600]{1,0:T(8,128)(2,1)}) %all-reduce.4.cloned.1.call-update) | async-done | bytes 2560016 | tf_op jit(solution)/shard_map/psum | solution.py:58
  414.1 4.6 %convert_multiply_fusion = f32[800,1600]{1,0:T(8,128)} fusion(bf16[800,1600]{1,0:T(8,128)(2,1)} %all-reduce.4.cloned.1.call-done), kind=kLoop, calls=%fused_computation.10 | loop fusion | flops 2560000 | bytes 7680000 | tf_op jit(solution)/shard_map/mul | solution.py:68
  (8 shorter events, 0.0 us)
Async XLA Ops:
  7.2 114.6 %all-gather.2.cloned.1.call-start = ((), (), s32[]{:S(2)}) async-start(), calls=%async_computation.1 | async-start | bytes 23961600 | tf_op jit(solution)/shard_map/all_gather | solution.py:41
  7.9 297.0 %reduce-scatter.2.cloned.1.call-start = ((), (), s32[]{:S(2)}) async-start(), calls=%async_computation.2 | async-start | bytes 23961600 | tf_op jit(solution)/shard_map/reduce_scatter | solution.py:50
  39.2 102.4 %copy-start = (bf16[384,1600]{0,1:T(8,128)(2,1)S(1)}, bf16[384,1600]{0,1:T(8,128)(2,1)}, u32[]{:S(2)}) copy-start(bf16[384,1600]{0,1:T(8,128)(2,1)} %param.6) | copy-start | bytes 3686404
  39.2 102.4 %copy-start.1 = (f32[1600]{0:T(1024)S(1)}, f32[1600]{0:T(1024)}, u32[]{:S(2)}) copy-start(f32[1600]{0:T(1024)} %param.7) | copy-start | bytes 19204
  159.4 254.7 %all-reduce.4.cloned.1.call-start = ((), (), s32[]{:S(2)}) async-start(), calls=%async_computation.3 | async-start | bytes 5324800 | tf_op jit(solution)/shard_map/psum | solution.py:58
Sparse Core Ops, SparseCore 0:
  9.9 111.7 all-gather.1
  159.5 145.3 reduce-scatter.1
  307.3 106.6 all-reduce.3
where the time goes:
time: 426 us; the launch traced here: 425 us
  waiting for transfers between devices  270 us (63%)
  blocking collectives  70.5 us (17%)
  matrix products  56 us (13%)
  between operations  14.4 us (3%)
  other arithmetic  11.5 us (3%)
    reduce_scatter x1, waiting for transfers between devices, local(): lax.psum_scatter(lax.dot_general(grad_low, normed, (((0,), (0,)), ((), ()...  145 us
    all_gather x1, waiting for transfers between devices, local(): lax.all_gather(up_weight, 'fsdp', axis=0, tiled=True)  82.5 us
    psum x1, blocking collectives, local(): lax.psum((jnp.sum(grad_pre, axis=0), jnp.sum(grad_norm * x_hat, axis=0)),...  44.5 us
    psum x1, waiting for transfers between devices, local(): weight_sum = lax.psum(weight_part, 'rep').astype(jnp.float32)  41.6 us
    unnamed x1, blocking collectives  26 us
    dot_general x1, matrix products, contract_last(): lax.dot_general(left, right, (((1,), (1,)), ((), ())), preferred_element_...  19.9 us
    dot_general x1, matrix products, local(): jnp.dot(grad_low, weight_all, preferred_element_type=jnp.float32)  18.3 us
    dot_general x1, matrix products, local(): lax.dot_general(grad_low, normed, (((0,), (0,)), ((), ())), preferred_ele...  17.7 us
  transfers between devices with their start and end apart: 3, of which 3 were waited for; matrix products, arithmetic and copies ran while one was open for 6% of the time, Pallas kernels for 0%

commit v1 on v0

--- a/solution.py
+++ b/solution.py
@@ -1,9 +1,25 @@
+import functools
 import math
 
 import jax
 import jax.numpy as jnp
 from jax import lax
+from jax.experimental import pallas as pl
+from jax.experimental.pallas import tpu as pltpu
 from jax.sharding import PartitionSpec as P
+
+CHUNKS = (160, 160, 160, 160, 160)
+ORDER = (
+    "O B0 B1 B3 ",
+    "W0 R0 W2 B2 ",
+    "W1 R1 S0 G ",
+    "T0 S1 B4 W3 ",
+    "T1 R2 W4 U0 ",
+    "R3 S2 G U1 ",
+    "S3 T2 R4 T3 ",
+    "U2 S4 T4 H ",
+    "U3 U4 ",
+)
 
 
 def normalize(tokens, norm_gain):
@@ -29,6 +45,583 @@
     return lax.dot_general(
         left, right, (((1,), (1,)), ((), ())), preferred_element_type=jnp.float32
     )
+
+
+def swap(value, bit):
+    return lax.ppermute(value, "fsdp", [(i, i ^ bit) for i in range(8)])
+
+
+def swap_core(value):
+    return swap(value, 1)
+
+
+def swap_x(value):
+    return swap(value, 2)
+
+
+def swap_y(value):
+    return swap(value, 4)
+
+
+LANES = 128
+
+
+def work_body(sizes, spots, width, *refs):
+    m = len(sizes)
+    place, normed_hbm, flipped_hbm, scale = refs[:4]
+    piece_hbm = refs[4 : 4 + m]
+    outs = refs[4 + m + 3 :]
+    states, low_hbm, grad_hbm = outs[:2], outs[3 : 3 + m], outs[3 + m : 3 + 2 * m]
+    normed, flipped, pre, cot, hid = outs[3 + 2 * m : 8 + 2 * m]
+    piece_v, low_v, grad_v = outs[8 + 2 * m : 11 + 2 * m]
+    main_sem, in_sem, cot_sem, out_sem = outs[11 + 2 * m :]
+    rows2 = normed.shape[0]
+    rows = rows2 // 2
+    depth = normed.shape[1]
+    block = depth // 4
+    begin = [sum(sizes[:j]) for j in range(m)]
+
+    def near(j):
+        return pl.ds(begin[j], sizes[j])
+
+    def spot(j):
+        start, side = spots[j]
+        return pl.ds(pl.multiple_of(start + width * (place[0] ^ side), 16), sizes[j])
+
+    copy = pltpu.make_async_copy
+    flipped_in = [
+        copy(flipped_hbm.at[pl.ds(i * block, block)], flipped.at[pl.ds(i * block, block)], main_sem.at[i])
+        for i in range(4)
+    ]
+    part = rows2 // 4
+    normed_in = [
+        copy(normed_hbm.at[pl.ds(i * part, part)], normed.at[pl.ds(i * part, part)], main_sem.at[4 + i])
+        for i in range(4)
+    ]
+    piece_in = [copy(piece_hbm[j], piece_v.at[near(j)], in_sem.at[j]) for j in range(m)]
+    cot_in = [
+        copy(states[i].at[spot(j)], cot.at[near(j), pl.ds(i * rows, rows)], cot_sem.at[2 * j + i])
+        for j in range(m)
+        for i in range(2)
+    ]
+    hid_out = [
+        copy(hid.at[near(j), pl.ds(i * rows, rows)], states[i].at[spot(j)], out_sem.at[4 * j + i])
+        for j in range(m)
+        for i in range(2)
+    ]
+    low_out = [copy(low_v.at[near(j)], low_hbm[j], out_sem.at[4 * j + 2]) for j in range(m)]
+    grad_out = [copy(grad_v.at[near(j)], grad_hbm[j], out_sem.at[4 * j + 3]) for j in range(m)]
+
+    piece_in[0].start()
+    for one in flipped_in:
+        one.start()
+    for one in cot_in[:2]:
+        one.start()
+    for one in normed_in:
+        one.start()
+    for j in range(1, m):
+        piece_in[j].start()
+        for one in cot_in[2 * j : 2 * j + 2]:
+            one.start()
+    for j in range(m):
+        size = sizes[j]
+        piece_in[j].wait()
+        if j == 0:
+            for one in flipped_in:
+                one.wait()
+        pre[:size, :] = jnp.dot(piece_v[near(j), :], flipped[...], preferred_element_type=jnp.float32)
+        for one in cot_in[2 * j : 2 * j + 2]:
+            one.wait()
+
+        @pl.loop(0, size // 16)
+        def _(strip):
+            here = pl.ds(pl.multiple_of(strip * 16, 16), 16)
+            there = pl.ds(pl.multiple_of(begin[j] + strip * 16, 16), 16)
+            for col in range(0, rows2, 2 * LANES):
+                cols = pl.ds(col, 2 * LANES)
+                gelu_out, slopes = activate(pre[here, cols])
+                factor = scale[:, cols]
+                hid[there, cols] = (gelu_out * factor).astype(jnp.bfloat16)
+                grad = cot[there, cols].astype(jnp.float32) * factor * slopes
+                low_v[there, cols] = grad.astype(jnp.bfloat16)
+
+        for one in hid_out[2 * j : 2 * j + 2]:
+            one.start()
+        low_out[j].start()
+        if j == 0:
+            for one in normed_in:
+                one.wait()
+        for col in range(0, depth, 4 * LANES):
+            cols = pl.ds(col, min(4 * LANES, depth - col))
+            grad_v[near(j), cols] = jnp.dot(
+                low_v[near(j), :], normed[:, cols], preferred_element_type=jnp.float32
+            ).astype(jnp.bfloat16)
+        grad_out[j].start()
+    for one in hid_out + low_out + grad_out:
+        one.wait()
+
+
+def call(body, operands, outs, aliases, scratch=(), limit=40):
+    spec = {
+        "hbm": pl.BlockSpec(memory_space=pltpu.HBM),
+        "vmem": pl.BlockSpec(memory_space=pltpu.VMEM),
+        "smem": pl.BlockSpec(memory_space=pltpu.SMEM),
+    }
+    return pl.pallas_call(
+        body,
+        out_shape=[jax.ShapeDtypeStruct(shape, dtype) for _, shape, dtype in outs],
+        in_specs=[spec[space] for space, _ in operands],
+        out_specs=[spec[space] for space, _, _ in outs],
+        scratch_shapes=list(scratch),
+        input_output_aliases=aliases,
+        compiler_params=pltpu.CompilerParams(vmem_limit_bytes=limit * 1024 * 1024),
+        cost_estimate=pl.CostEstimate(flops=0, bytes_accessed=0, transcendentals=0),
+    )(*[value for _, value in operands])
+
+
+def work(pieces, spots, width, place, normed, flipped, scale, states, token):
+    sizes = [piece.shape[0] for piece in pieces]
+    m, total = len(sizes), sum(sizes)
+    rows2, depth = normed.shape
+    low = jnp.bfloat16
+    results = call(
+        functools.partial(work_body, sizes, spots, width),
+        [("smem", place), ("hbm", normed), ("hbm", flipped), ("vmem", scale)]
+        + [("hbm", piece) for piece in pieces]
+        + [("hbm", states[0]), ("hbm", states[1]), ("hbm", token)],
+        [("hbm", states[0].shape, low), ("hbm", states[1].shape, low)]
+        + [("hbm", token.shape, token.dtype)]
+        + [("hbm", (size, rows2), low) for size in sizes]
+        + [("hbm", (size, depth), low) for size in sizes],
+        {4 + m: 0, 5 + m: 1, 6 + m: 2},
+        [
+            pltpu.VMEM((rows2, depth), low),
+            pltpu.VMEM((depth, rows2), low),
+            pltpu.VMEM((max(sizes), rows2), jnp.float32),
+            pltpu.VMEM((total, rows2), low),
+            pltpu.VMEM((total, rows2), low),
+            pltpu.VMEM((total, depth), low),
+            pltpu.VMEM((total, rows2), low),
+            pltpu.VMEM((total, depth), low),
+            pltpu.SemaphoreType.DMA((8,)),
+            pltpu.SemaphoreType.DMA((m,)),
+            pltpu.SemaphoreType.DMA((2 * m,)),
+            pltpu.SemaphoreType.DMA((4 * m,)),
+        ],
+    )
+    return results[:2], results[2], results[3 : 3 + m], results[3 + m :]
+
+
+def total_body(count, extra, start, scale, *refs):
+    terms = refs[:count]
+    outs = refs[-6:-4] if scale else refs[-4:-3]
+    values, result, sem = refs[-3:]
+    ending = refs[-4]
+    size, depth = terms[0].shape
+    wide = result.shape[1]
+    moves = [
+        pltpu.make_async_copy(terms[i], values.at[i], sem.at[i]) for i in range(count)
+    ]
+    for one in moves:
+        one.start()
+    for one in moves:
+        one.wait()
+
+    @pl.loop(0, size // 16)
+    def _(strip):
+        here = pl.ds(pl.multiple_of(strip * 16, 16), 16)
+        total = values[0, here, :].astype(jnp.float32)
+        for i in range(1, count):
+            total = total + values[i, here, :].astype(jnp.float32)
+        if scale:
+            total = total.astype(jnp.bfloat16).astype(jnp.float32) * scale
+            ending[here, :] = total[:, depth - LANES :]
+            total = total[:, :wide]
+        result[here, :] = total.astype(result.dtype)
+
+    if extra:
+        tail = pl.ds(depth - LANES, LANES)
+        result[:, tail] = (result[:, tail].astype(jnp.float32) + refs[count][...]).astype(result.dtype)
+    if scale:
+        here = pl.ds(start, size)
+        back = [
+            pltpu.make_async_copy(result, outs[0].at[here], sem.at[0]),
+            pltpu.make_async_copy(ending, outs[1].at[here], sem.at[1]),
+        ]
+    else:
+        back = [pltpu.make_async_copy(result, outs[0], sem.at[0])]
+    for one in back:
+        one.start()
+    for one in back:
+        one.wait()
+
+
+def total_of(operands, token, extra=None):
+    shape = operands[0].shape
+    given = [("hbm", value) for value in operands]
+    if extra is not None:
+        given.append(("vmem", extra))
+    results = call(
+        functools.partial(total_body, len(operands), extra is not None, 0, None),
+        given + [("hbm", token)],
+        [("hbm", token.shape, token.dtype), ("hbm", shape, jnp.bfloat16)],
+        {len(given): 0},
+        [
+            pltpu.VMEM((len(operands),) + shape, jnp.bfloat16),
+            pltpu.VMEM(shape, jnp.bfloat16),
+            pltpu.SemaphoreType.DMA((len(operands),)),
+        ],
+        limit=16,
+    )
+    return results[1], results[0]
+
+
+def finish_of(operands, results, shapes, start, scale, token, before):
+    shape = operands[0].shape
+    given = [("hbm", value) for value in operands] + [("hbm", value) for value in before]
+    aliases = {len(given): 0}
+    given.append(("hbm", token))
+    for i, value in enumerate(results):
+        aliases[len(given)] = 1 + i
+        given.append(("hbm", value))
+    outs = call(
+        functools.partial(total_body, len(operands), False, start, scale),
+        given,
+        [("hbm", token.shape, token.dtype)] + [("hbm", one, jnp.float32) for one in shapes],
+        aliases,
+        [
+            pltpu.VMEM((shape[0], LANES), jnp.float32),
+            pltpu.VMEM((len(operands),) + shape, jnp.bfloat16),
+            pltpu.VMEM((shape[0], shapes[0][1]), jnp.float32),
+            pltpu.SemaphoreType.DMA((len(operands),)),
+        ],
+        limit=16,
+    )
+    return outs[1:], outs[0]
+
+
+def spread_body(sizes, more, last, *refs):
+    m = len(sizes)
+    low_hbm, piece_hbm = refs[:m], refs[m : 2 * m]
+    acc, low_v, piece_v, sem = refs[-4:]
+    begin = [sum(sizes[:j]) for j in range(m)]
+    copy = pltpu.make_async_copy
+    moves = []
+    for j in range(m):
+        here = pl.ds(begin[j], sizes[j])
+        moves.append(copy(low_hbm[j], low_v.at[here], sem.at[2 * j]))
+        moves.append(copy(piece_hbm[j], piece_v.at[here], sem.at[2 * j + 1]))
+    if more:
+        fetch = copy(refs[2 * m], acc, sem.at[2 * m])
+        fetch.start()
+    for one in moves:
+        one.start()
+    width = acc.shape[1]
+    for group in range(0, m, 4):
+        for one in moves[2 * group : 2 * group + 8]:
+            one.wait()
+        end = min(group + 4, m) - 1
+        here = pl.ds(begin[group], begin[end] + sizes[end] - begin[group])
+        turned = low_v[here, :].T
+        if more and not group:
+            fetch.wait()
+        for col in range(0, width, 4 * LANES):
+            cols = pl.ds(col, min(4 * LANES, width - col))
+            part = jnp.dot(turned, piece_v[here, cols], preferred_element_type=jnp.float32)
+            if group or more:
+                part = part + acc[:, cols]
+            acc[:, cols] = part
+    if not last:
+        out = copy(acc, refs[-5], sem.at[0])
+        out.start()
+        out.wait()
+        return
+    tokens, token_out, gain = refs[2 * m + more : 2 * m + more + 2], refs[-8], refs[-5]
+    own, peer = refs[-7:-5]
+    rows, depth = tokens[0].shape
+    out = [
+        copy(acc.at[pl.ds(0, rows)], own, sem.at[0]),
+        copy(acc.at[pl.ds(rows, rows)], peer, sem.at[1]),
+    ]
+    for one in out:
+        one.start()
+    gain[...] = jnp.zeros_like(gain)
+    for index, source in enumerate(tokens):
+
+        @pl.loop(0, rows // 16)
+        def _(strip):
+            values = source[pl.ds(pl.multiple_of(strip * 16, 16), 16), :].astype(jnp.float32)
+            x_hat = values * lax.rsqrt(jnp.mean(values * values, axis=1, keepdims=True) + 1e-06)
+            here = pl.ds(pl.multiple_of(index * rows + strip * 16, 16), 16)
+            product = acc[here, :depth] * x_hat
+            gain[...] += product[:8] + product[8:]
+
+    for one in out:
+        one.wait()
+
+
+def spread(lows, pieces, token, former=None, tokens=None):
+    sizes = [low.shape[0] for low in lows]
+    m, total = len(sizes), sum(sizes)
+    rows2, depth = lows[0].shape[1], pieces[0].shape[1]
+    given = [("hbm", low) for low in lows] + [("hbm", piece) for piece in pieces]
+    if former is not None:
+        given.append(("hbm", former))
+    outs = [("hbm", token.shape, token.dtype)]
+    if tokens is None:
+        outs.append(("hbm", (rows2, depth), jnp.float32))
+    else:
+        given += [("vmem", one) for one in tokens]
+        rows, narrow = tokens[0].shape
+        outs += [("hbm", (rows, depth), jnp.float32)] * 2 + [("vmem", (8, narrow), jnp.float32)]
+    results = call(
+        functools.partial(spread_body, sizes, int(former is not None), tokens is not None),
+        given + [("hbm", token)],
+        outs,
+        {len(given): 0},
+        [
+            pltpu.VMEM((rows2, depth), jnp.float32),
+            pltpu.VMEM((total, rows2), jnp.bfloat16),
+            pltpu.VMEM((total, depth), jnp.bfloat16),
+            pltpu.SemaphoreType.DMA((2 * m + 1,)),
+        ],
+        limit=48,
+    )
+    return results[1:], results[0]
+
+
+def pack_body(sizes, weight, bias, token, token_out, *outs):
+    depth = weight.shape[1]
+    full = outs[0].shape[1]
+    lane = lax.broadcasted_iota(jnp.int32, (16, LANES), 1) + (full - LANES)
+    start = 0
+    for size, out in zip(sizes, outs):
+        out[:, :depth] = weight[pl.ds(start, size), :]
+        for row in range(0, size, 16):
+            column = jnp.broadcast_to(bias[:, start + row : start + row + 16], (LANES, 16)).T
+            last = out[row : row + 16, full - LANES :].astype(jnp.float32)
+            last = jnp.where(lane < depth, last, jnp.where(lane == depth, column, 0.0))
+            out[row : row + 16, full - LANES :] = last.astype(jnp.bfloat16)
+        start += size
+
+
+def pack(weight, bias, token):
+    depth = weight.shape[1]
+    full = depth + -depth % LANES
+    results = call(
+        functools.partial(pack_body, CHUNKS),
+        [("vmem", weight), ("vmem", bias.astype(jnp.float32)[None, :]), ("hbm", token)],
+        [("hbm", token.shape, token.dtype)]
+        + [("vmem", (size, full), jnp.bfloat16) for size in CHUNKS],
+        {2: 0},
+    )
+    return results[1:], results[0]
+
+
+def ranges(units, width):
+    for first in range(0, units, LANES):
+        at, cuts = first, []
+        while at < min(first + LANES, units):
+            stop = min(first + LANES, units, (at // width + 1) * width)
+            cuts.append((at // width, at % width, at - first, stop - at))
+            at = stop
+        yield first, cuts
+
+
+def turn_body(width, place, cot, token, token_out, own, peer):
+    core = place[1]
+    for first, cuts in ranges(cot.shape[1], width):
+        block = cot[:, first : first + LANES].T
+        for shard, offset, at, size in cuts:
+            to = pl.ds((shard // 2) * width + offset, size)
+            mine = core == shard % 2
+
+            @pl.when(mine)
+            def _():
+                own[to, :] = block[at : at + size]
+
+            @pl.when(jnp.logical_not(mine))
+            def _():
+                peer[to, :] = block[at : at + size]
+
+
+def turn(cotangent, width, place, token):
+    rows, units = cotangent.shape
+    half = ("vmem", (units // 2, rows), jnp.bfloat16)
+    results = call(
+        functools.partial(turn_body, width),
+        [("smem", place), ("vmem", cotangent), ("hbm", token)],
+        [("hbm", token.shape, token.dtype), half, half],
+        {2: 0},
+    )
+    return results[1], results[2], results[0]
+
+
+def back_body(width, place, own, peer, token, token_out, out):
+    core = place[1]
+    for first, cuts in ranges(out.shape[1], width):
+        blocks = []
+        for shard, offset, at, size in cuts:
+            to = pl.ds((shard // 2) * width + offset, size)
+            blocks.append(jnp.where(core == shard % 2, own[to, :], peer[to, :]))
+        block = blocks[0] if len(blocks) == 1 else jnp.concatenate(blocks, axis=0)
+        out[:, first : first + LANES] = block.T
+
+
+def back(own, peer, width, place, token):
+    units, rows = 2 * own.shape[0], own.shape[1]
+    results = call(
+        functools.partial(back_body, width),
+        [("smem", place), ("vmem", own), ("vmem", peer), ("hbm", token)],
+        [("hbm", token.shape, token.dtype), ("vmem", (rows, units), jnp.bfloat16)],
+        {3: 0},
+    )
+    return results[1], results[0]
+
+
+def norm_body(own, peer, gain, token, token_out, normed, flipped):
+    rows, depth = own.shape
+    full = normed.shape[1]
+    spare = full - depth // LANES * LANES
+    lane = lax.broadcasted_iota(jnp.int32, (LANES, LANES), 1) + (full - LANES)
+    for index, source in enumerate((own, peer)):
+
+        @pl.loop(0, rows // LANES)
+        def _(strip):
+            values = source[pl.ds(pl.multiple_of(strip * LANES, LANES), LANES), :].astype(jnp.float32)
+            mean_sq = jnp.mean(values * values, axis=1, keepdims=True)
+            value = values * lax.rsqrt(mean_sq + 1e-06) * gain[...]
+            to = pl.ds(pl.multiple_of(index * rows + strip * LANES, LANES), LANES)
+            normed[to, :depth] = value.astype(jnp.bfloat16)
+            last = normed[to, full - LANES :]
+            last = jnp.where(lane < depth, last, jnp.where(lane == depth, 1.0, 0.0).astype(jnp.bfloat16))
+            normed[to, full - LANES :] = last
+            for col in range(0, full, LANES):
+                flipped[col : col + LANES, to] = normed[to, col : col + LANES].T
+
+
+def norm(tokens, peer, norm_gain, token):
+    rows, depth = tokens.shape
+    full = depth + -depth % LANES
+    results = call(
+        norm_body,
+        [("vmem", tokens), ("vmem", peer), ("vmem", norm_gain[None, :]), ("hbm", token)],
+        [
+            ("hbm", token.shape, token.dtype),
+            ("vmem", (2 * rows, full), jnp.bfloat16),
+            ("vmem", (full, 2 * rows), jnp.bfloat16),
+        ],
+        {3: 0},
+    )
+    return results[1], results[2], results[0]
+
+
+def swap_plane(value, bit=1):
+    return lax.ppermute(value, "rep", [(i, i ^ bit) for i in range(4)])
+
+
+def paired(tokens, norm_gain, up_weight, up_bias, keep_mask, cotangent):
+    rows, depth = tokens.shape
+    width = up_weight.shape[0]
+    index = lax.axis_index("fsdp")
+    place = jnp.stack([index >> 1, index & 1]).astype(jnp.int32)
+    inv_root = 1.0 / math.sqrt(rows * 32)
+    count = len(CHUNKS)
+    starts = [sum(CHUNKS[:c]) for c in range(count)]
+    spare = -depth % LANES
+
+    token = jnp.zeros((8, LANES), jnp.float32)
+    own, token = pack(up_weight, up_bias, token)
+    from_x = [swap_x(piece) for piece in own]
+    from_y = [swap_y(piece) for piece in own]
+    from_d = [swap_x(from_y[c]) if c % 2 == 0 else swap_y(from_x[c]) for c in range(count)]
+
+    tokens_peer = swap_core(tokens)
+    scale_own = row_scales(keep_mask, rows)
+    scale = jnp.concatenate([scale_own, swap_core(scale_own)])[None, :]
+    cot_own, cot_peer, token = turn(cotangent, width, place, token)
+    normed, flipped, token = norm(tokens, tokens_peer, norm_gain, token)
+    states = [cot_own, swap_core(cot_peer)]
+
+    pieces = {}
+    for c in range(count):
+        pieces["O", c], pieces["X", c], pieces["Y", c] = own[c], from_x[c], from_y[c]
+        pieces["D", c] = from_d[c]
+    side = {"O": 0, "X": 1, "Y": 2, "D": 3}
+    lows, grads, sent_x, sent_y, relayed = {}, {}, {}, {}, {}
+    summed, across, used, results, former = {}, {}, set(), (), None
+    hidden = grad_in = None
+
+    def run(keys):
+        nonlocal states, token
+        spots = [(starts[c], side[kind]) for kind, c in keys]
+        states, token, low, grad = work(
+            [pieces[key] for key in keys], spots, width, place, normed, flipped, scale, states, token
+        )
+        for key, one, other in zip(keys, low, grad):
+            lows[key], grads[key] = one, other
+
+    for task in "".join(ORDER).split():
+        kind, c = task[0], int(task[1:] or 0)
+        even = c % 2 == 0
+        if kind == "W":
+            run([("X", c), ("Y", c)])
+            if even:
+                sent_y[c] = swap_y(grads["Y", c])
+            else:
+                sent_x[c] = swap_x(grads["X", c])
+        elif kind == "B":
+            run([("D", c)])
+            relayed[c] = swap_y(grads["D", c]) if even else swap_x(grads["D", c])
+        elif kind == "O":
+            run([("O", k) for k in range(count)])
+        elif kind == "R":
+            value, token = total_of([grads["X" if even else "Y", c], relayed[c]], token)
+            if even:
+                sent_x[c] = swap_x(value)
+            else:
+                sent_y[c] = swap_y(value)
+        elif kind == "S":
+            extra = None
+            if c == count - 1:
+                lanes = jnp.pad(gain.reshape(depth // 16, 16), ((0, CHUNKS[c] - depth // 16), (0, 0)))
+                extra = jnp.pad(lanes, ((0, 0), (LANES - 16, 0)))
+            summed[c], token = total_of([grads["O", c], sent_x[c], sent_y[c]], token, extra)
+            across[c] = swap_plane(summed[c], 1)
+        elif kind == "T":
+            summed[c], token = total_of([summed[c], across[c]], token)
+            across[c] = swap_plane(summed[c], 2)
+        elif kind == "U":
+            shapes = [(width, depth), (width, LANES)]
+            before = () if hidden is None else (hidden, grad_in)
+            results, token = finish_of(
+                [summed[c], across[c]], results, shapes, starts[c], inv_root, token, before
+            )
+        elif kind == "G":
+            keys = [key for key in lows if key not in used]
+            used.update(keys)
+            given = [lows[key] for key in keys], [pieces[key] for key in keys]
+            if len(used) < 4 * count:
+                (former,), token = spread(*given, token, former)
+            else:
+                (whole, peer, gain), token = spread(*given, token, former, (tokens, tokens_peer))
+                peer = swap_core(peer)
+                gain = jnp.sum(gain, axis=0)
+                gain = gain + swap_core(gain)
+                gain = gain + swap_x(gain)
+                gain = gain + swap_y(gain)
+        elif kind == "H":
+            hidden, token = back(states[0], swap_core(states[1]), width, place, token)
+            x_hat, inv_rms, _ = normalize(tokens, norm_gain)
+            scaled = (whole + peer)[:, :depth] * norm_gain[None, :]
+            grad_in = (
+                inv_rms * (scaled - x_hat * jnp.mean(scaled * x_hat, axis=1, keepdims=True))
+            ).astype(jnp.bfloat16)
+
+    grad_weight, tail = results
+    grad_bias = tail[:, LANES - spare]
+    grad_gain = tail[starts[-1] : starts[-1] + depth // 16, LANES - 16 :].reshape(depth)
+    return (hidden, grad_in, grad_weight, grad_bias, grad_gain)
 
 
 def local(tokens, norm_gain, up_weight, up_bias, keep_mask, cotangent):
@@ -69,8 +662,9 @@
 
 
 def solution(mesh):
+    body = paired if (mesh.shape["fsdp"], mesh.shape["rep"]) == (8, 4) else local
     return jax.shard_map(
-        local,
+        body,
         mesh=mesh,
         in_specs=(
             P(("fsdp", "rep"), None),

time: 426 us -> 331 us (0.78)
  waiting for transfers between devices: 270 us -> 100 us
  Pallas kernels: 0 us -> 137 us
  blocking collectives: 70.5 us -> 0 us
  matrix products: 56 us -> 0 us
  starting transfers between devices: 0.3 us -> 46.6 us
  local copies, waits for them, and re-layouts: 2.28 us -> 34.6 us
  between operations: 14.4 us -> 2.37 us
  other arithmetic: 11.5 us -> 5.75 us
    reduce_scatter x1 -> x0, waiting for transfers between devices: 145 us -> none  [local(): lax.psum_scatter(lax.dot_general(grad_low, normed, (((0,), (0,)), ((), ()...]
    pallas_call x0 -> x37, Pallas kernels: none -> 137 us  [call(): pl.pallas_call(body, out_shape=[jax.ShapeDtypeStruct(shape, dtype) for _,...]
    ppermute x0 -> x48, waiting for transfers between devices: none -> 100 us  [the longest x10 76.8 us: swap_plane(): return lax.ppermute(value, 'rep', [(i, i ^ bit) for i in range(4)])]
    all_gather x1 -> x0, waiting for transfers between devices: 82.5 us -> none  [local(): lax.all_gather(up_weight, 'fsdp', axis=0, tiled=True)]
    dot_general x3 -> x0, matrix products: 56 us -> none  [the longest x1 19.9 us: contract_last(): lax.dot_general(left, right, (((1,), (1,)), ((), ())), preferred_element_...]
    ppermute x0 -> x48, starting transfers between devices: none -> 46.6 us  [the longest x38 38.4 us: swap(): return lax.ppermute(value, 'fsdp', [(i, i ^ bit) for i in range(8)])]
    psum x1 -> x0, blocking collectives: 44.5 us -> none  [local(): lax.psum((jnp.sum(grad_pre, axis=0), jnp.sum(grad_norm * x_hat, axis=0)),...]
    psum x1 -> x0, waiting for transfers between devices: 41.6 us -> none  [local(): weight_sum = lax.psum(weight_part, 'rep').astype(jnp.float32)]
  transfers between devices with their start and end apart: 3 -> 48, of which waited for: 3 -> 15; matrix products, arithmetic and copies ran while one was open for 6% -> 4% of each run, Pallas kernels for 0% -> 35%
where the time goes in v1:
time: 331 us; the launch traced here: 327 us
  Pallas kernels  137 us (41%)
  waiting for transfers between devices  100 us (30%)
  starting transfers between devices  46.6 us (14%)
  local copies, waits for them, and re-layouts  34.6 us (10%)
  other arithmetic  5.75 us (2%)
    pallas_call x37, Pallas kernels, call(): pl.pallas_call(body, out_shape=[jax.ShapeDtypeStruct(shape, dtype) for _,...  137 us
    ppermute x10, waiting for transfers between devices, swap_plane(): return lax.ppermute(value, 'rep', [(i, i ^ bit) for i in range(4)])  76.8 us
    ppermute x38, starting transfers between devices, swap(): return lax.ppermute(value, 'fsdp', [(i, i ^ bit) for i in range(8)])  38.4 us
    unnamed x176, local copies, waits for them, and re-layouts  29.4 us
    ppermute x38, waiting for transfers between devices, swap(): return lax.ppermute(value, 'fsdp', [(i, i ^ bit) for i in range(8)])  23.5 us
    ppermute x10, starting transfers between devices, swap_plane(): return lax.ppermute(value, 'rep', [(i, i ^ bit) for i in range(4)])  8.25 us
  transfers between devices with their start and end apart: 48, of which 15 were waited for; matrix products, arithmetic and copies ran while one was open for 4% of the time, Pallas kernels for 35%

profile of v1, /device:TPU:0, one launch (start us, length us, event | category | flops | bytes accessed | tf_op | source)
XLA Modules:
  0.0 326.8 jit_solution(17124664058836225708)
XLA Ops:
  9.0 6.6 %shard_map.102 = (f32[8,128]{1,0:T(8,128)S(1)}, bf16[3200,384]{1,0:T(8,128)(2,1)S(1)}, bf16[3200,384]{1,0:T(8,128)(2,1)}) custom-call(s32[2]{0:T(128)S(1)} %pad_add_fusion.place.refs_0_, bf16[384,6400]{1,0:T(8,128)(2,1)S(1)} %copy-done.6, f32[8,128]{1,0:T(8,128)S(1)} %get-tuple-element.142.token), custom_call_target="tpu_custom_call", output_to_operand_aliasing={{0}: (2, {})} | custom-call | tf_op jit(solution)/shard_map/pallas_call | solution.py:170
  23.2 8.2 %collective-permute-done.13.refs_5_.refs_24_ = bf16[160,1664]{1,0:T(8,128)(2,1)} collective-permute-done((bf16[160,1664]{1,0:T(8,128)(2,1)S(1)}, bf16[160,1664]{1,0:T(8,128)(2,1)}, u32[]{:S(2)}, u32[]{:S(2)}) %collective-permute-start.13) | collective-permute-done | bytes 532512 | tf_op jit(solution)/shard_map/ppermute | solution.py:51
  51.3 14.3 %shard_map.104 = (bf16[3200,384]{1,0:T(8,128)(2,1)S(1)}, bf16[3200,384]{1,0:T(8,128)(2,1)}, f32[8,128]{1,0:T(8,128)S(1)}, bf16[160,768]{1,0:T(8,128)(2,1)S(1)}, ...) custom-call(s32[2]{0:T(128)S(1)} %pad_add_fusion.place.refs_0_, ...), custom_call_target="tpu_custom_call", output_to_operand_aliasing={{0}: (9, {}), {1}: (10, {}), {2}: (11, {})} | custom-call | tf_op jit(solution)/shard_map/pallas_call | solution.py:170
  66.5 4.5 %shard_map.105 = (bf16[3200,384]{1,0:T(8,128)(2,1)S(1)}, bf16[3200,384]{1,0:T(8,128)(2,1)}, f32[8,128]{1,0:T(8,128)S(1)}, bf16[160,768]{1,0:T(8,128)(2,1)S(1)}, bf16[160,1664]{1,0:T(8,128)(2,1)S(1)}) custom-call(s32[2]{0:T(128)S(1)} %pad_add_fusion.place.refs_0_, ...), custom_call_target="tpu_custom_call", output_to_operand_aliasing={{0}: (5, {}), {1}: (6, {}), {2}: (7, {})} | custom-call | tf_op jit(solution)/shard_map/pallas_call | solution.py:170
  73.2 4.4 %shard_map.106 = (bf16[3200,384]{1,0:T(8,128)(2,1)S(1)}, bf16[3200,384]{1,0:T(8,128)(2,1)}, f32[8,128]{1,0:T(8,128)S(1)}, bf16[160,768]{1,0:T(8,128)(2,1)S(1)}, bf16[160,1664]{1,0:T(8,128)(2,1)S(1)}) custom-call(s32[2]{0:T(128)S(1)} %pad_add_fusion.place.refs_0_, ...), custom_call_target="tpu_custom_call", output_to_operand_aliasing={{0}: (5, {}), {1}: (6, {}), {2}: (7, {})} | custom-call | tf_op jit(solution)/shard_map/pallas_call | solution.py:170
  80.4 4.7 %shard_map.107 = (bf16[3200,384]{1,0:T(8,128)(2,1)S(1)}, bf16[3200,384]{1,0:T(8,128)(2,1)}, f32[8,128]{1,0:T(8,128)S(1)}, bf16[160,768]{1,0:T(8,128)(2,1)S(1)}, bf16[160,1664]{1,0:T(8,128)(2,1)S(1)}) custom-call(s32[2]{0:T(128)S(1)} %pad_add_fusion.place.refs_0_, ...), custom_call_target="tpu_custom_call", output_to_operand_aliasing={{0}: (5, {}), {1}: (6, {}), {2}: (7, {})} | custom-call | tf_op jit(solution)/shard_map/pallas_call | solution.py:170
  86.9 6.8 %shard_map.108 = (bf16[3200,384]{1,0:T(8,128)(2,1)S(1)}, bf16[3200,384]{1,0:T(8,128)(2,1)}, f32[8,128]{1,0:T(8,128)S(1)}, bf16[160,768]{1,0:T(8,128)(2,1)S(1)}, ...) custom-call(s32[2]{0:T(128)S(1)} %pad_add_fusion.place.refs_0_, ...), custom_call_target="tpu_custom_call", output_to_operand_aliasing={{0}: (6, {}), {1}: (7, {}), {2}: (8, {})} | custom-call | tf_op jit(solution)/shard_map/pallas_call | solution.py:170
  97.5 6.9 %shard_map.110 = (bf16[3200,384]{1,0:T(8,128)(2,1)S(1)}, bf16[3200,384]{1,0:T(8,128)(2,1)}, f32[8,128]{1,0:T(8,128)S(1)}, bf16[160,768]{1,0:T(8,128)(2,1)S(1)}, ...) custom-call(s32[2]{0:T(128)S(1)} %pad_add_fusion.place.refs_0_, ...), custom_call_target="tpu_custom_call", output_to_operand_aliasing={{0}: (6, {}), {1}: (7, {}), {2}: (8, {})} | custom-call | tf_op jit(solution)/shard_map/pallas_call | solution.py:170
  105.1 4.5 %shard_map.111 = (bf16[3200,384]{1,0:T(8,128)(2,1)S(1)}, bf16[3200,384]{1,0:T(8,128)(2,1)}, f32[8,128]{1,0:T(8,128)S(1)}, bf16[160,768]{1,0:T(8,128)(2,1)S(1)}, bf16[160,1664]{1,0:T(8,128)(2,1)S(1)}) custom-call(s32[2]{0:T(128)S(1)} %pad_add_fusion.place.refs_0_, ...), custom_call_target="tpu_custom_call", output_to_operand_aliasing={{0}: (5, {}), {1}: (6, {}), {2}: (7, {})} | custom-call | tf_op jit(solution)/shard_map/pallas_call | solution.py:170
  110.5 6.8 %shard_map.112 = (bf16[3200,384]{1,0:T(8,128)(2,1)S(1)}, bf16[3200,384]{1,0:T(8,128)(2,1)}, f32[8,128]{1,0:T(8,128)S(1)}, bf16[160,768]{1,0:T(8,128)(2,1)S(1)}, ...) custom-call(s32[2]{0:T(128)S(1)} %pad_add_fusion.place.refs_0_, ...), custom_call_target="tpu_custom_call", output_to_operand_aliasing={{0}: (6, {}), {1}: (7, {}), {2}: (8, {})} | custom-call | tf_op jit(solution)/shard_map/pallas_call | solution.py:170
  129.6 17.4 %shard_map.115 = (f32[8,128]{1,0:T(8,128)S(1)}, f32[768,1664]{1,0:T(8,128)}) custom-call(bf16[160,768]{1,0:T(8,128)(2,1)S(1)} %copy-done.38, bf16[160,768]{1,0:T(8,128)(2,1)S(1)} %copy-done.40, bf16[160,768]{1,0:T(8,128)(2,1)S(1)} %copy-done.42, bf16[160,768]{1,0:T(8,128)(2,1)S(1)} %copy-done.44, ...), custom_call_target="tpu_custom_call", output_to_operand_aliasing={{0}: (30, {})} | custom-call | tf_op jit(solution)/shard_map/pallas_call | solution.py:170
  154.0 4.5 %shard_map.118 = (bf16[3200,384]{1,0:T(8,128)(2,1)S(1)}, bf16[3200,384]{1,0:T(8,128)(2,1)}, f32[8,128]{1,0:T(8,128)S(1)}, bf16[160,768]{1,0:T(8,128)(2,1)S(1)}, bf16[160,1664]{1,0:T(8,128)(2,1)S(1)}) custom-call(s32[2]{0:T(128)S(1)} %pad_add_fusion.place.refs_0_, ...), custom_call_target="tpu_custom_call", output_to_operand_aliasing={{0}: (5, {}), {1}: (6, {}), {2}: (7, {})} | custom-call | tf_op jit(solution)/shard_map/pallas_call | solution.py:170
  160.5 6.8 %shard_map.119 = (bf16[3200,384]{1,0:T(8,128)(2,1)S(1)}, bf16[3200,384]{1,0:T(8,128)(2,1)}, f32[8,128]{1,0:T(8,128)S(1)}, bf16[160,768]{1,0:T(8,128)(2,1)S(1)}, ...) custom-call(s32[2]{0:T(128)S(1)} %pad_add_fusion.place.refs_0_, ...), custom_call_target="tpu_custom_call", output_to_operand_aliasing={{0}: (6, {}), {1}: (7, {}), {2}: (8, {})} | custom-call | tf_op jit(solution)/shard_map/pallas_call | solution.py:170
  171.4 7.9 %shard_map.122 = (bf16[3200,384]{1,0:T(8,128)(2,1)S(1)}, bf16[3200,384]{1,0:T(8,128)(2,1)}, f32[8,128]{1,0:T(8,128)S(1)}, bf16[160,768]{1,0:T(8,128)(2,1)S(1)}, ...) custom-call(s32[2]{0:T(128)S(1)} %pad_add_fusion.place.refs_0_, ...), custom_call_target="tpu_custom_call", output_to_operand_aliasing={{0}: (6, {}), {1}: (7, {}), {2}: (8, {})} | custom-call | tf_op jit(solution)/shard_map/pallas_call | solution.py:170
  179.4 6.0 %collective-permute-done.32.refs_1_ = bf16[160,1664]{1,0:T(8,128)(2,1)S(1)} collective-permute-done((bf16[160,1664]{1,0:T(8,128)(2,1)S(1)}, bf16[160,1664]{1,0:T(8,128)(2,1)S(1)}, u32[]{:S(2)}, u32[]{:S(2)}) %collective-permute-start.32) | collective-permute-done | bytes 532512 | tf_op jit(solution)/shard_map/ppermute | solution.py:520
  188.4 13.2 %shard_map.126 = (f32[8,128]{1,0:T(8,128)S(1)}, f32[384,1664]{1,0:T(8,128)}, f32[384,1664]{1,0:T(8,128)}, f32[8,1600]{1,0:T(8,128)S(1)}) custom-call(bf16[160,768]{1,0:T(8,128)(2,1)S(1)} %copy-done.58, bf16[160,768]{1,0:T(8,128)(2,1)S(1)} %copy-done.64, bf16[160,768]{1,0:T(8,128)(2,1)S(1)} %copy-done.66, ...), custom_call_target="tpu_custom_call", output_to_operand_aliasing={{0}: (13, {})} | custom-call | tf_op jit(solution)/shard_map/pallas_call | solution.py:170
  207.9 9.1 %collective-permute-done.34.refs_1_ = bf16[160,1664]{1,0:T(8,128)(2,1)S(1)} collective-permute-done((bf16[160,1664]{1,0:T(8,128)(2,1)}, bf16[160,1664]{1,0:T(8,128)(2,1)S(1)}, u32[]{:S(2)}, u32[]{:S(2)}) %collective-permute-start.34) | collective-permute-done | bytes 532512 | tf_op jit(solution)/shard_map/ppermute | solution.py:51
  217.7 12.8 %collective-permute-done.36.refs_1_ = bf16[160,1664]{1,0:T(8,128)(2,1)S(1)} collective-permute-done((bf16[160,1664]{1,0:T(8,128)(2,1)S(1)}, bf16[160,1664]{1,0:T(8,128)(2,1)S(1)}, u32[]{:S(2)}, u32[]{:S(2)}) %collective-permute-start.36) | collective-permute-done | bytes 532512 | tf_op jit(solution)/shard_map/ppermute | solution.py:520
  234.3 7.6 %collective-permute-done.33.refs_1_ = bf16[160,1664]{1,0:T(8,128)(2,1)S(1)} collective-permute-done((bf16[160,1664]{1,0:T(8,128)(2,1)}, bf16[160,1664]{1,0:T(8,128)(2,1)S(1)}, u32[]{:S(2)}, u32[]{:S(2)}) %collective-permute-start.33) | collective-permute-done | bytes 532512 | tf_op jit(solution)/shard_map/ppermute | solution.py:520
  246.9 7.0 %collective-permute-done.43.refs_1_ = bf16[160,1664]{1,0:T(8,128)(2,1)S(1)} collective-permute-done((bf16[160,1664]{1,0:T(8,128)(2,1)S(1)}, bf16[160,1664]{1,0:T(8,128)(2,1)S(1)}, u32[]{:S(2)}, u32[]{:S(2)}) %collective-permute-start.43) | collective-permute-done | bytes 532512 | tf_op jit(solution)/shard_map/ppermute | solution.py:520
  258.6 10.5 %collective-permute-done.42.refs_1_ = bf16[160,1664]{1,0:T(8,128)(2,1)} collective-permute-done((bf16[160,1664]{1,0:T(8,128)(2,1)S(1)}, bf16[160,1664]{1,0:T(8,128)(2,1)}, u32[]{:S(2)}, u32[]{:S(2)}) %collective-permute-start.42) | collective-permute-done | bytes 532512 | tf_op jit(solution)/shard_map/ppermute | solution.py:520
  276.1 20.3 %collective-permute-done.44.refs_1_ = bf16[160,1664]{1,0:T(8,128)(2,1)S(1)} collective-permute-done((bf16[160,1664]{1,0:T(8,128)(2,1)S(1)}, bf16[160,1664]{1,0:T(8,128)(2,1)S(1)}, u32[]{:S(2)}, u32[]{:S(2)}) %collective-permute-start.44) | collective-permute-done | bytes 532512 | tf_op jit(solution)/shard_map/ppermute | solution.py:520
  296.9 5.5 %shard_map.135 = (f32[8,128]{1,0:T(8,128)S(1)}, bf16[384,6400]{1,0:T(8,128)(2,1)}) custom-call(s32[2]{0:T(128)S(1)} %pad_add_fusion.place.refs_0_, bf16[3200,384]{1,0:T(8,128)(2,1)S(1)} %get-tuple-element.221.own, bf16[3200,384]{1,0:T(8,128)(2,1)} %collective-permute-done.27.peer, f32[8,128]{1,0:T(8,128)S(1)} %get-tuple-element.265.token), custom_call_target="tpu_custom_call", output_to_operand_aliasing={{0}: (3, {})} | custom-call | tf_op jit(solution)/shard_map/pallas_call | solution.py:170
  312.2 9.6 %collective-permute-done.46.refs_1_ = bf16[160,1664]{1,0:T(8,128)(2,1)S(1)} collective-permute-done((bf16[160,1664]{1,0:T(8,128)(2,1)S(1)}, bf16[160,1664]{1,0:T(8,128)(2,1)S(1)}, u32[]{:S(2)}, u32[]{:S(2)}) %collective-permute-start.46) | collective-permute-done | bytes 532512 | tf_op jit(solution)/shard_map/ppermute | solution.py:520
  (310 shorter events, 118.6 us)
Async XLA Ops:
  15.6 34.2 %collective-permute-start.17 = (bf16[3200,384]{1,0:T(8,128)(2,1)}, bf16[3200,384]{1,0:T(8,128)(2,1)}, u32[]{:S(2)}, u32[]{:S(2)}) collective-permute-start(bf16[3200,384]{1,0:T(8,128)(2,1)} %get-tuple-element.152), channel_id=1, source_target_pairs={{0,4},{4,0},{8,12},{12,8},{16,20},{20,16},{24,28},{28,24},{1,5},{5... | collective-permute-start | bytes 7372808 | tf_op jit(solution)/shard_map/ppermute | solution.py:51
  22.1 26.1 %collective-permute-start.4 = (bf16[160,1664]{1,0:T(8,128)(2,1)}, bf16[160,1664]{1,0:T(8,128)(2,1)}, u32[]{:S(2)}, u32[]{:S(2)}) collective-permute-start(bf16[160,1664]{1,0:T(8,128)(2,1)} %get-tuple-element.147.refs_7_.refs_18_), channel_id=1, source_target_pairs={{0,8},{4,12},{8,0},{12,4},{16,24},{20,28},{24,16},{28,20},{1,9},{5... | collective-permute-start | bytes 1597448 | tf_op jit(solution)/shard_map/ppermute | solution.py:51
  31.4 35.1 %collective-permute-start.16 = (bf16[160,1664]{1,0:T(8,128)(2,1)}, bf16[160,1664]{1,0:T(8,128)(2,1)S(1)}, u32[]{:S(2)}, u32[]{:S(2)}) collective-permute-start(bf16[160,1664]{1,0:T(8,128)(2,1)} %collective-permute-done.13.refs_5_.refs_24_), channel_id=1, source_target_pairs={{0,8},{4,12},{8,0},{12,4},{16,24},{20,28},{24,16},{28,20},{1,9},{5... | collective-permute-start | bytes 1597448 | tf_op jit(solution)/shard_map/ppermute | solution.py:51
  34.4 38.4 %collective-permute-start.15 = (bf16[160,1664]{1,0:T(8,128)(2,1)}, bf16[160,1664]{1,0:T(8,128)(2,1)}, u32[]{:S(2)}, u32[]{:S(2)}) collective-permute-start(bf16[160,1664]{1,0:T(8,128)(2,1)} %collective-permute-done.7.refs_4_.refs_28_), channel_id=1, source_target_pairs={{0,16},{4,20},{8,24},{12,28},{16,0},{20,4},{24,8},{28,12},{1,17},{... | collective-permute-start | bytes 1597448 | tf_op jit(solution)/shard_map/ppermute | solution.py:51
  37.6 49.0 %collective-permute-start.12 = (bf16[160,1664]{1,0:T(8,128)(2,1)S(1)}, bf16[160,1664]{1,0:T(8,128)(2,1)}, u32[]{:S(2)}, u32[]{:S(2)}) collective-permute-start(bf16[160,1664]{1,0:T(8,128)(2,1)S(1)} %get-tuple-element.150.refs_4_.refs_15_), channel_id=1, source_target_pairs={{0,8},{4,12},{8,0},{12,4},{16,24},{20,28},{24,16},{28,20},{1,9},{5... | collective-permute-start | bytes 1597448 | tf_op jit(solution)/shard_map/ppermute | solution.py:51
  48.2 30.2 %collective-permute-start.9 = (bf16[160,1664]{1,0:T(8,128)(2,1)S(1)}, bf16[160,1664]{1,0:T(8,128)(2,1)S(1)}, u32[]{:S(2)}, u32[]{:S(2)}) collective-permute-start(bf16[160,1664]{1,0:T(8,128)(2,1)S(1)} %copy-done.15), channel_id=1, source_target_pairs={{0,16},{4,20},{8,24},{12,28},{16,0},{20,4},{24,8},{28,12},{1,17},{... | collective-permute-start | bytes 1597448 | tf_op jit(solution)/shard_map/ppermute | solution.py:51
  49.8 29.0 %collective-permute-start.14 = (bf16[160,1664]{1,0:T(8,128)(2,1)}, bf16[160,1664]{1,0:T(8,128)(2,1)S(1)}, u32[]{:S(2)}, u32[]{:S(2)}) collective-permute-start(bf16[160,1664]{1,0:T(8,128)(2,1)} %collective-permute-done.4.refs_4_.refs_6_), channel_id=1, source_target_pairs={{0,16},{4,20},{8,24},{12,28},{16,0},{20,4},{24,8},{28,12},{1,17},{... | collective-permute-start | bytes 1597448 | tf_op jit(solution)/shard_map/ppermute | solution.py:51
  78.4 32.0 %collective-permute-start.8 = (bf16[160,1664]{1,0:T(8,128)(2,1)}, bf16[160,1664]{1,0:T(8,128)(2,1)S(1)}, u32[]{:S(2)}, u32[]{:S(2)}) collective-permute-start(bf16[160,1664]{1,0:T(8,128)(2,1)} %get-tuple-element.148.refs_5_.refs_16_), channel_id=1, source_target_pairs={{0,16},{4,20},{8,24},{12,28},{16,0},{20,4},{24,8},{28,12},{1,17},{... | collective-permute-start | bytes 1597448 | tf_op jit(solution)/shard_map/ppermute | solution.py:51
  78.7 25.8 %collective-permute-start.10 = (bf16[160,1664]{1,0:T(8,128)(2,1)S(1)}, bf16[160,1664]{1,0:T(8,128)(2,1)S(1)}, u32[]{:S(2)}, u32[]{:S(2)}) collective-permute-start(bf16[160,1664]{1,0:T(8,128)(2,1)S(1)} %collective-permute-done.9.refs_5_.refs_26_), channel_id=1, source_target_pairs={{0,8},{4,12},{8,0},{12,4},{16,24},{20,28},{24,16},{28,20},{1,9},{5... | collective-permute-start | bytes 1597448 | tf_op jit(solution)/shard_map/ppermute | solution.py:51
  86.6 30.8 %collective-permute-start.20 = (bf16[160,1664]{1,0:T(8,128)(2,1)S(1)}, bf16[160,1664]{1,0:T(8,128)(2,1)S(1)}, u32[]{:S(2)}, u32[]{:S(2)}) collective-permute-start(bf16[160,1664]{1,0:T(8,128)(2,1)S(1)} %get-tuple-element.183), channel_id=1, source_target_pairs={{0,8},{4,12},{8,0},{12,4},{16,24},{20,28},{24,16},{28,20},{1,9},{5... | collective-permute-start | bytes 1597448 | tf_op jit(solution)/shard_map/ppermute | solution.py:51
  119.1 27.9 %collective-permute-start.24 = (bf16[160,1664]{1,0:T(8,128)(2,1)S(1)}, bf16[160,1664]{1,0:T(8,128)(2,1)}, u32[]{:S(2)}, u32[]{:S(2)}) collective-permute-start(bf16[160,1664]{1,0:T(8,128)(2,1)S(1)} %get-tuple-element.190.refs_0_), channel_id=1, source_target_pairs={{0,1},{1,0},{2,3},{3,2},{4,5},{5,4},{6,7},{7,6},{8,9},{9,8},{10,11... | collective-permute-start | bytes 1597448 | tf_op jit(solution)/shard_map/ppermute | solution.py:520
  120.7 27.8 %collective-permute-start.21 = (bf16[160,1664]{1,0:T(8,128)(2,1)}, bf16[160,1664]{1,0:T(8,128)(2,1)S(1)}, u32[]{:S(2)}, u32[]{:S(2)}) collective-permute-start(bf16[160,1664]{1,0:T(8,128)(2,1)} %get-tuple-element.185), channel_id=1, source_target_pairs={{0,16},{4,20},{8,24},{12,28},{16,0},{20,4},{24,8},{28,12},{1,17},{... | collective-permute-start | bytes 1597448 | tf_op jit(solution)/shard_map/ppermute | solution.py:51
  122.2 26.2 %collective-permute-start.19 = (bf16[160,1664]{1,0:T(8,128)(2,1)}, bf16[160,1664]{1,0:T(8,128)(2,1)}, u32[]{:S(2)}, u32[]{:S(2)}) collective-permute-start(bf16[160,1664]{1,0:T(8,128)(2,1)} %get-tuple-element.181), channel_id=1, source_target_pairs={{0,8},{4,12},{8,0},{12,4},{16,24},{20,28},{24,16},{28,20},{1,9},{5... | collective-permute-start | bytes 1597448 | tf_op jit(solution)/shard_map/ppermute | solution.py:51
  122.8 37.2 %collective-permute-start.5 = (bf16[160,1664]{1,0:T(8,128)(2,1)}, bf16[160,1664]{1,0:T(8,128)(2,1)S(1)}, u32[]{:S(2)}, u32[]{:S(2)}) collective-permute-start(bf16[160,1664]{1,0:T(8,128)(2,1)} %get-tuple-element.147.refs_7_.refs_18_), channel_id=1, source_target_pairs={{0,16},{4,20},{8,24},{12,28},{16,0},{20,4},{24,8},{28,12},{1,17},{... | collective-permute-start | bytes 1597448 | tf_op jit(solution)/shard_map/ppermute | solution.py:51
  123.3 29.2 %collective-permute-start.6 = (bf16[160,1664]{1,0:T(8,128)(2,1)S(1)}, bf16[160,1664]{1,0:T(8,128)(2,1)S(1)}, u32[]{:S(2)}, u32[]{:S(2)}) collective-permute-start(bf16[160,1664]{1,0:T(8,128)(2,1)S(1)} %collective-permute-done.3.refs_5_.refs_9_), channel_id=1, source_target_pairs={{0,8},{4,12},{8,0},{12,4},{16,24},{20,28},{24,16},{28,20},{1,9},{5... | collective-permute-start | bytes 1597448 | tf_op jit(solution)/shard_map/ppermute | solution.py:51
  152.5 34.1 %collective-permute-start.31 = (bf16[160,1664]{1,0:T(8,128)(2,1)S(1)}, bf16[160,1664]{1,0:T(8,128)(2,1)S(1)}, u32[]{:S(2)}, u32[]{:S(2)}) collective-permute-start(bf16[160,1664]{1,0:T(8,128)(2,1)S(1)} %copy-done.74), channel_id=1, source_target_pairs={{0,8},{4,12},{8,0},{12,4},{16,24},{20,28},{24,16},{28,20},{1,9},{5... | collective-permute-start | bytes 1597448 | tf_op jit(solution)/shard_map/ppermute | solution.py:51
  160.0 27.0 %collective-permute-start.30 = (bf16[160,1664]{1,0:T(8,128)(2,1)S(1)}, bf16[160,1664]{1,0:T(8,128)(2,1)S(1)}, u32[]{:S(2)}, u32[]{:S(2)}) collective-permute-start(bf16[160,1664]{1,0:T(8,128)(2,1)S(1)} %copy-done.76), channel_id=1, source_target_pairs={{0,16},{4,20},{8,24},{12,28},{16,0},{20,4},{24,8},{28,12},{1,17},{... | collective-permute-start | bytes 1597448 | tf_op jit(solution)/shard_map/ppermute | solution.py:51
  201.6 100.9 %collective-permute-start.45 = (f32[384,1664]{1,0:T(8,128)}, f32[384,1664]{1,0:T(8,128)}, u32[]{:S(2)}, u32[]{:S(2)}) collective-permute-start(f32[384,1664]{1,0:T(8,128)} %get-tuple-element.268), channel_id=1, source_target_pairs={{0,4},{4,0},{8,12},{12,8},{16,20},{20,16},{24,28},{28,24},{1,5},{5... | collective-permute-start | bytes 7667720 | tf_op jit(solution)/shard_map/ppermute | solution.py:51
  201.7 95.2 %collective-permute-start.27 = (bf16[3200,384]{1,0:T(8,128)(2,1)}, bf16[3200,384]{1,0:T(8,128)(2,1)}, u32[]{:S(2)}, u32[]{:S(2)}) collective-permute-start(bf16[3200,384]{1,0:T(8,128)(2,1)} %get-tuple-element.222), channel_id=1, source_target_pairs={{0,4},{4,0},{8,12},{12,8},{16,20},{20,16},{24,28},{28,24},{1,5},{5... | collective-permute-start | bytes 7372808 | tf_op jit(solution)/shard_map/ppermute | solution.py:51
  203.8 26.6 %collective-permute-start.36 = (bf16[160,1664]{1,0:T(8,128)(2,1)S(1)}, bf16[160,1664]{1,0:T(8,128)(2,1)S(1)}, u32[]{:S(2)}, u32[]{:S(2)}) collective-permute-start(bf16[160,1664]{1,0:T(8,128)(2,1)S(1)} %get-tuple-element.239.refs_0_), channel_id=1, source_target_pairs={{0,2},{1,3},{2,0},{3,1},{4,6},{5,7},{6,4},{7,5},{8,10},{9,11},{10,... | collective-permute-start | bytes 1597448 | tf_op jit(solution)/shard_map/ppermute | solution.py:520
  217.0 24.9 %collective-permute-start.33 = (bf16[160,1664]{1,0:T(8,128)(2,1)}, bf16[160,1664]{1,0:T(8,128)(2,1)S(1)}, u32[]{:S(2)}, u32[]{:S(2)}) collective-permute-start(bf16[160,1664]{1,0:T(8,128)(2,1)} %copy-done.31), channel_id=1, source_target_pairs={{0,1},{1,0},{2,3},{3,2},{4,5},{5,4},{6,7},{7,6},{8,9},{9,8},{10,11... | collective-permute-start | bytes 1597448 | tf_op jit(solution)/shard_map/ppermute | solution.py:520
  245.5 26.0 %collective-permute-start.38 = (bf16[160,1664]{1,0:T(8,128)(2,1)}, bf16[160,1664]{1,0:T(8,128)(2,1)}, u32[]{:S(2)}, u32[]{:S(2)}) collective-permute-start(bf16[160,1664]{1,0:T(8,128)(2,1)} %get-tuple-element.254), channel_id=1, source_target_pairs={{0,16},{4,20},{8,24},{12,28},{16,0},{20,4},{24,8},{28,12},{1,17},{... | collective-permute-start | bytes 1597448 | tf_op jit(solution)/shard_map/ppermute | solution.py:51
  273.6 37.3 %collective-permute-start.47 = (bf16[160,1664]{1,0:T(8,128)(2,1)S(1)}, bf16[160,1664]{1,0:T(8,128)(2,1)S(1)}, u32[]{:S(2)}, u32[]{:S(2)}) collective-permute-start(bf16[160,1664]{1,0:T(8,128)(2,1)S(1)} %get-tuple-element.270.refs_0_), channel_id=1, source_target_pairs={{0,2},{1,3},{2,0},{3,1},{4,6},{5,7},{6,4},{7,5},{8,10},{9,11},{10,... | collective-permute-start | bytes 1597448 | tf_op jit(solution)/shard_map/ppermute | solution.py:520
  296.8 25.0 %collective-permute-start.46 = (bf16[160,1664]{1,0:T(8,128)(2,1)S(1)}, bf16[160,1664]{1,0:T(8,128)(2,1)S(1)}, u32[]{:S(2)}, u32[]{:S(2)}) collective-permute-start(bf16[160,1664]{1,0:T(8,128)(2,1)S(1)} %get-tuple-element.269.refs_0_), channel_id=1, source_target_pairs={{0,2},{1,3},{2,0},{3,1},{4,6},{5,7},{6,4},{7,5},{8,10},{9,11},{10,... | collective-permute-start | bytes 1597448 | tf_op jit(solution)/shard_map/ppermute | solution.py:520
  (111 other events, 918.9 us)
